TPU v7x, 32 devices: a whole 2x2x4 slice. The times are simulated.
32 devices in a mesh: groups: 2 (over y), rows: 8 (over z, x), sub: 2 (over core).
Axes of the slice: x: 2, y: 2, z: 4, core: 2. Of those that a mesh axis runs over, the one named last changes fastest.
Arguments:
- coupling: bfloat16 [131072, 128], P(('groups', 'rows', 'sub')), parts along dimension 0, may hold values from 0.009 to 110
- tile_vals: bfloat16 [1024, 6, 128, 128], P(('groups', 'rows', 'sub')), parts along dimension 0, may hold values from -0.02734375 to 0.02734375
- tile_cols: int32 [1024, 6], P(('groups', 'rows', 'sub')), parts along dimension 0, may hold values from 0 to 511, as said below
- cluster_graph: int32 [256, 128], P('groups'), parts along dimension 0, may hold values from 0 to 3
- cluster_mass: float32 [256], P('groups'), parts along dimension 0, may hold values from 0.25 to 4
Outputs:
- log_coupling: float32 [131072, 128], P(('groups', 'rows', 'sub')), parts along dimension 0
There are 2 independent parts, one for each index of `groups`. A program takes and returns all parts, laid end to end along the dimension named above; each array names one. Nothing has to cross between parts.
Inputs may be any that keep to these rules, and one draw needn't show every extreme that they name: `tile_cols`: within each device's rows of 32 block rows, a slot below 4 names a column block held by the same device or by the device just before or after it along rows+sub. Over the slots from 4 on, the block rows of one device name column blocks held by any one device at most 4 times, and some device exactly 4 times.
All inputs are finite; a program needn't handle non-finite values.
Results may differ from a plain program's by a relative error of at most 0.0003.
Values may be sent and summed in bfloat16 or wider, within the bound.
A program may use at most 128 MiB of HBM per device.

v0:
```python
import jax
import jax.numpy as jnp
from jax import lax
from jax.sharding import PartitionSpec as P

NEAR = 4


eta_step = 2.0
relax_power = 0.5


def padded(cells, sides, width):
    for axis, dim in sides:
        count = lax.axis_size(axis)
        ends = count - 1
        head = lax.slice_in_dim(cells, 0, width, axis=dim)
        tail = lax.slice_in_dim(cells, cells.shape[dim] - width, cells.shape[dim], axis=dim)
        cells = jnp.concatenate(
            [
                lax.ppermute(tail, axis, [(i, (i + 1) % count) for i in range(ends)]),
                cells,
                lax.ppermute(head, axis, [((i + 1) % count, i) for i in range(ends)]),
            ],
            axis=dim,
        )
    return cells


def local(coupling, tile_vals, tile_cols, cluster_graph, cluster_mass):
    shards = lax.axis_size(("rows", "sub"))
    my_index = lax.axis_index(("rows", "sub"))
    blocks_dev = tile_cols.shape[0]
    tile_size = tile_vals.shape[2]
    clusters = coupling.shape[1]
    far_slots = tile_cols.shape[1] - NEAR
    nodes_total = blocks_dev * tile_size * shards
    blocks_local = coupling.reshape(blocks_dev, tile_size, clusters)
    window = padded(coupling, ((("rows", "sub"), 0),), blocks_dev * tile_size)
    window = window.reshape(3 * blocks_dev, tile_size, clusters)
    near_index = tile_cols[:, :NEAR] - (my_index * blocks_dev - blocks_dev)
    spread = jnp.zeros((blocks_dev, tile_size, clusters), jnp.float32)
    for slot_id in range(NEAR):
        picked = jnp.take(window, near_index[:, slot_id], axis=0)
        spread = spread + jnp.einsum(
            "nij,njk->nik", tile_vals[:, slot_id], picked, preferred_element_type=jnp.float32
        )
    far_count = blocks_dev * far_slots
    capacity = (far_count + shards - 1) // shards
    far_cols = tile_cols[:, NEAR:].reshape(far_count)
    far_owner = far_cols // blocks_dev
    far_local = far_cols % blocks_dev
    owner_hits = (far_owner[:, None] == jnp.arange(shards, dtype=jnp.int32)[None, :]).astype(
        jnp.int32
    )
    earlier = jnp.cumsum(owner_hits, axis=0) - owner_hits
    far_slot = jnp.sum(earlier * owner_hits, axis=1)
    requests = jnp.zeros((shards, capacity), jnp.int32).at[far_owner, far_slot].set(far_local)
    found = jnp.take(
        blocks_local,
        lax.all_to_all(requests, ("rows", "sub"), split_axis=0, concat_axis=0, tiled=True),
        axis=0,
    )
    fetched = lax.all_to_all(found, ("rows", "sub"), split_axis=0, concat_axis=0, tiled=True)
    far_blocks = fetched[far_owner, far_slot]
    far_tiles = tile_vals[:, NEAR:].reshape(far_count, tile_size, tile_size)
    far_terms = jnp.einsum(
        "nij,njk->nik", far_tiles, far_blocks, preferred_element_type=jnp.float32
    )
    spread = spread + jnp.sum(far_terms.reshape(blocks_dev, far_slots, tile_size, clusters), axis=1)
    spread = spread.reshape(blocks_dev * tile_size, clusters)
    graph = cluster_graph.astype(jnp.float32)
    affinity = jnp.dot(spread, graph.T / clusters, precision=lax.Precision.HIGHEST)
    whole = coupling.astype(jnp.float32)
    mass_part = jnp.sum(whole, axis=0) / nodes_total
    boosted = jnp.log(whole) + 2.0 * eta_step * affinity
    boost_part = jnp.sum(jnp.exp(boosted), axis=0) / nodes_total
    colmass, boost_mass = lax.psum((mass_part, boost_part), ("rows", "sub"))
    pull = jnp.dot(graph * graph, colmass, precision=lax.Precision.HIGHEST) / clusters
    logits = boosted - eta_step * pull[None, :]
    log_new = jnp.log(boost_mass) - eta_step * pull
    shifted = logits + relax_power * (jnp.log(cluster_mass) - log_new)[None, :]
    return shifted - jnp.log(jnp.sum(jnp.exp(shifted), axis=1, keepdims=True))


def solution(mesh):
    return jax.shard_map(
        local,
        mesh=mesh,
        in_specs=(
            P(("groups", "rows", "sub"), None),
            P(("groups", "rows", "sub"), None, None, None),
            P(("groups", "rows", "sub"), None),
            P("groups", None),
            P("groups"),
        ),
        out_specs=P(("groups", "rows", "sub"), None),
        check_vma=False,
    )
```

profile of v0, /device:TPU:0, one launch (start us, length us, event | category | flops | bytes accessed | tf_op | source)
XLA Modules:
  0.0 164.6 jit_solution(341923318796550742)
XLA Ops:
  0.0 0.8 slice.42
  0.9 0.1 reshape.172
  1.0 0.1 reshape.171
  1.3 0.2 select_reduce_fusion
  1.5 3.5 %scatter_fusion = s32[16,4]{0,1:T(4,128)S(1)} fusion(s32[16,4]{0,1:T(4,128)S(1)} %broadcast_in_dim.33, s32[64]{0:T(128)S(1)} %fusion.34, s32[64]{0:T(128)S(1)} %get-tuple-element.24), kind=kCustom, calls=%fused_computation.6 | custom fusion | bytes 1280 | tf_op jit(solution)/shard_map/scatter | solution.py:58
  5.1 13.6 %all_to_all.20 = s32[16,1,4]{2,1,0:T(1,128)S(1)} all-to-all(s32[16,1,4]{2,1,0:T(1,128)S(1)} %copy.29), channel_id=1, replica_groups=mesh['groups'=2,'rows'=8,'sub'=2] {'rows','sub'}, dimensions={0} | all-to-all | bytes 512 | tf_op jit(solution)/shard_map/all_to_all | solution.py:61
  18.9 0.1 copy.31
  19.0 0.9 gather_fusion
  20.0 1.6 broadcast_select_fusion
  21.6 4.6 %all-to-all-start.1 = ((bf16[16,4,128,128]{3,2,1,0:T(8,128)(2,1)}), bf16[16,4,128,128]{3,2,1,0:T(8,128)(2,1)}, u32[]{:S(2)}, u32[]{:S(2)}) async-start(bf16[16,4,128,128]{3,2,1,0:T(8,128)(2,1)} %broadcast_select_fusion), calls=%async_computation.1 | async-start | bytes 4194304 | tf_op jit(solution)/shard_map/all_to_all | solution.py:64
  26.2 2.2 %collective-permute-start = (bf16[4096,128]{1,0:T(8,128)(2,1)S(1)}, bf16[4096,128]{1,0:T(8,128)(2,1)S(1)}, u32[]{:S(2)}, u32[]{:S(2)}) collective-permute-start(bf16[4096,128]{1,0:T(8,128)(2,1)S(1)} %copy-done), channel_id=1, source_target_pairs={{0,1},{1,2},{2,3},{3,4},{4,5},{5,6},{6,7},{7,8},{8,9},{9,10},{10,1... | collective-permute-start | bytes 3145736 | tf_op jit(solution)/shard_map/ppermute | solution.py:21
  28.3 1.3 collective-permute-start.1
  29.7 0.6 convert_reduce_fusion
  30.3 0.3 collective-permute-done
  30.5 3.4 %collective-permute-done.1 = bf16[4096,128]{1,0:T(8,128)(2,1)S(1)} collective-permute-done((bf16[4096,128]{1,0:T(8,128)(2,1)S(1)}, bf16[4096,128]{1,0:T(8,128)(2,1)S(1)}, u32[]{:S(2)}, u32[]{:S(2)}) %collective-permute-start.1) | collective-permute-done | bytes 1048608 | tf_op jit(solution)/shard_map/ppermute | solution.py:23
  34.0 16.4 %pad_maximum_fusion = bf16[12288,128]{1,0:T(8,128)(2,1)} fusion(bf16[4096,128]{1,0:T(8,128)(2,1)S(1)} %collective-permute-done.1, bf16[4096,128]{1,0:T(8,128)(2,1)S(1)} %copy-done, bf16[4096,128]{1,0:T(8,128)(2,1)S(1)} %collective-permute-done), kind=kLoop, calls=%fused_computation.10 | loop fusion | flops 9437184 | bytes 6291456 | tf_op jit(solution)/shard_map/concatenate | solution.py:19
  50.4 3.6 %gather_fusion.4 = bf16[32,128,128]{2,1,0:T(8,128)(2,1)} fusion(bf16[96,128,128]{2,1,0:T(8,128)(2,1)} %bitcast.80, s32[1024]{0:T(1024)S(1)} %get-tuple-element.30), kind=kCustom, calls=%fused_computation.2.clone | custom fusion | bytes 2097280 | tf_op jit(solution)/shard_map/jit(_take)/gather | solution.py:44
  54.0 3.6 %gather_fusion.3 = bf16[32,128,128]{2,1,0:T(8,128)(2,1)} fusion(bf16[96,128,128]{2,1,0:T(8,128)(2,1)} %bitcast.81, s32[1024]{0:T(1024)S(1)} %get-tuple-element.31), kind=kCustom, calls=%fused_computation.1.clone | custom fusion | bytes 2097280 | tf_op jit(solution)/shard_map/jit(_take)/gather | solution.py:44
  57.6 3.7 %gather_fusion.2 = bf16[32,128,128]{2,1,0:T(8,128)(2,1)} fusion(bf16[96,128,128]{2,1,0:T(8,128)(2,1)} %bitcast.82, s32[1024]{0:T(1024)S(1)} %pad_clamp_fusion.4), kind=kCustom, calls=%fused_computation.clone | custom fusion | bytes 2097280 | tf_op jit(solution)/shard_map/jit(_take)/gather | solution.py:44
  61.3 3.5 %gather_fusion.5 = bf16[32,128,128]{2,1,0:T(8,128)(2,1)} fusion(bf16[96,128,128]{2,1,0:T(8,128)(2,1)} %bitcast.83, s32[1024]{0:T(1024)S(1)} %pad_clamp_fusion.1), kind=kCustom, calls=%fused_computation.3.clone | custom fusion | bytes 2097280 | tf_op jit(solution)/shard_map/jit(_take)/gather | solution.py:44
  64.9 3.5 %fusion.4 = f32[32,128,128]{1,2,0:T(8,128)} fusion(bf16[32,128,128]{2,1,0:T(8,128)(2,1)} %gather_fusion.4, bf16[32,6,128,128]{3,2,1,0:T(8,128)(2,1)} %param.8, pred[32]{0:T(512)(128)(4,1)S(1)} %get-tuple-element.18), kind=kOutput, calls=%fused_computation.22 | convolution fusion | flops 134742016 | bytes 4194336 | tf_op jit(solution)/shard_map/nij,njk->nik/dot_general | solution.py:45
  68.4 3.5 %fusion.6 = f32[32,128,128]{1,2,0:T(8,128)} fusion(bf16[32,128,128]{2,1,0:T(8,128)(2,1)} %gather_fusion.3, bf16[32,6,128,128]{3,2,1,0:T(8,128)(2,1)} %param.8, pred[32]{0:T(512)(128)(4,1)S(1)} %get-tuple-element.20), kind=kOutput, calls=%fused_computation.24 | convolution fusion | flops 134742016 | bytes 4194336 | tf_op jit(solution)/shard_map/nij,njk->nik/dot_general | solution.py:45
  71.9 1.9 %fusion.8 = f32[32,128,128]{1,2,0:T(8,128)} fusion(bf16[32,128,128]{2,1,0:T(8,128)(2,1)S(1)} %copy-done.2, bf16[32,6,128,128]{3,2,1,0:T(8,128)(2,1)S(1)} %bitcast.85, pred[32]{0:T(512)(128)(4,1)S(1)} %get-tuple-element.22), kind=kOutput, calls=%fused_computation.26 | convolution fusion | flops 134742016 | bytes 4194816 | tf_op jit(solution)/shard_map/nij,njk->nik/dot_general | solution.py:45
  73.8 3.9 %gather_fusion.1 = bf16[64,128,128]{2,1,0:T(8,128)(2,1)} fusion(bf16[16,4,128,128]{3,2,1,0:T(8,128)(2,1)} %all-to-all-done.1, s32[64]{0:T(128)S(1)} %get-tuple-element.16), kind=kCustom, calls=%fused_computation.5 | custom fusion | bytes 4194816 | tf_op jit(solution)/shard_map/gather | solution.py:65
  77.7 4.6 %bitcast_reduce_fusion = f32[32,128,128]{1,2,0:T(8,128)} fusion(bf16[64,128,128]{2,1,0:T(8,128)(2,1)} %gather_fusion.1, bf16[64,128,128]{2,1,0:T(8,128)(2,1)S(1)} %bitcast.86), kind=kOutput, calls=%fused_computation.9 | convolution fusion | flops 268959744 | bytes 6291456 | tf_op jit(solution)/shard_map/nij,njk->nik/dot_general | solution.py:67
  82.3 3.0 %copy.35 = f32[32,128,128]{2,1,0:T(8,128)} copy(f32[32,128,128]{1,2,0:T(8,128)} %bitcast_reduce_fusion) | data formatting | bytes 4194304 | tf_op jit(solution)/shard_map/reduce_sum | solution.py:70
  85.4 4.2 %bitcast_add_fusion = f32[32,128,128]{2,1,0:T(8,128)S(1)} fusion(f32[32,128,128]{2,1,0:T(8,128)} %copy.35, f32[32,128,128]{1,2,0:T(8,128)S(1)} %copy-done.1, f32[32,128,128]{1,2,0:T(8,128)} %fusion.8, f32[32,128,128]{1,2,0:T(8,128)} %fusion.6, bf16[32,128,128]{2,1,0:T(8,128)(2,1)} %gather_fusion.5, bf16[32,6,128,128]{3,2,1,0:T(8,128)(2,1)} %param.8, ...), kind=kOutput, calls=%fused_computation.13 | convolution fusion | flops 136839168 | bytes 12582944 | tf_op jit(solution)/shard_map/nij,njk->nik/dot_general | solution.py:45
  89.6 2.1 %exponential_reduce_fusion.1 = (f32[128]{0:T(128)S(1)}, f32[4096,128]{1,0:T(8,128)S(1)}) fusion(f32[4096,128]{1,0:T(8,128)S(1)} %bitcast.87, s32[128,128]{1,0:T(8,128)S(1)} %copy-done.3, bf16[4096,128]{1,0:T(8,128)(2,1)S(1)} %copy-done), kind=kOutput, calls=%fused_computation.15 | convolution fusion | flops 807436160 | bytes 5308928 | tf_op jit(solution)/shard_map/dot_general | solution.py:73
  91.7 70.3 %all-reduce = (f32[128]{0:T(128)S(1)}, f32[128]{0:T(128)S(1)}) all-reduce(f32[128]{0:T(128)S(1)} %broadcast_multiply_fusion.1, f32[128]{0:T(128)S(1)} %broadcast_multiply_fusion), channel_id=1, replica_groups=mesh['groups'=2,'rows'=8,'sub'=2] {'rows','sub'}, use_global_device_ids=true, to_apply=%region_5.7 | all-reduce | flops 256 | bytes 2048 | tf_op jit(solution)/shard_map/psum | solution.py:78
  162.0 0.2 subtract_multiply_fusion
  162.2 0.7 exponential_reduce_fusion
  162.9 1.7 %fusion.1 = f32[4096,128]{1,0:T(8,128)} fusion(f32[4096,128]{1,0:T(8,128)S(1)} %get-tuple-element.27, f32[4096]{0:T(1024)S(1)} %log.20, f32[128]{0:T(128)S(1)} %get-tuple-element.28, f32[128]{0:T(128)S(1)} %get-tuple-element.29), kind=kLoop, calls=%fused_computation.18 | loop fusion | flops 1572864 | bytes 4211712 | tf_op jit(solution)/shard_map/sub | solution.py:83
  (42 shorter events, 0.8 us)
Async XLA Ops:
  0.0 19.0 %copy-start = (bf16[4096,128]{1,0:T(8,128)(2,1)S(1)}, bf16[4096,128]{1,0:T(8,128)(2,1)}, u32[]{:S(2)}) copy-start(bf16[4096,128]{1,0:T(8,128)(2,1)} %param.7) | copy-start | bytes 3145732
  21.6 8.1 %copy-start.4 = (s32[32,6]{0,1:T(8,128)S(1)}, s32[32,6]{0,1:T(8,128)}, u32[]{:S(2)}) copy-start(s32[32,6]{0,1:T(8,128)} %param.9) | copy-start | bytes 2308
  21.6 52.2 %all-to-all-start.1 = ((bf16[16,4,128,128]{3,2,1,0:T(8,128)(2,1)}), bf16[16,4,128,128]{3,2,1,0:T(8,128)(2,1)}, u32[]{:S(2)}, u32[]{:S(2)}) async-start(bf16[16,4,128,128]{3,2,1,0:T(8,128)(2,1)} %broadcast_select_fusion), calls=%async_computation.1 | async-start | bytes 4194304 | tf_op jit(solution)/shard_map/all_to_all | solution.py:64
  26.2 4.4 %collective-permute-start = (bf16[4096,128]{1,0:T(8,128)(2,1)S(1)}, bf16[4096,128]{1,0:T(8,128)(2,1)S(1)}, u32[]{:S(2)}, u32[]{:S(2)}) collective-permute-start(bf16[4096,128]{1,0:T(8,128)(2,1)S(1)} %copy-done), channel_id=1, source_target_pairs={{0,1},{1,2},{2,3},{3,4},{4,5},{5,6},{6,7},{7,8},{8,9},{9,10},{10,1... | collective-permute-start | bytes 3145736 | tf_op jit(solution)/shard_map/ppermute | solution.py:21
  28.3 5.6 %collective-permute-start.1 = (bf16[4096,128]{1,0:T(8,128)(2,1)S(1)}, bf16[4096,128]{1,0:T(8,128)(2,1)S(1)}, u32[]{:S(2)}, u32[]{:S(2)}) collective-permute-start(bf16[4096,128]{1,0:T(8,128)(2,1)S(1)} %copy-done), channel_id=1, source_target_pairs={{1,0},{2,1},{3,2},{4,3},{5,4},{6,5},{7,6},{8,7},{9,8},{10,9},{11,1... | collective-permute-start | bytes 3145736 | tf_op jit(solution)/shard_map/ppermute | solution.py:23
  57.6 14.3 %slice-start = ((s8[6291456]{0:T(1024)(128)(4,1)}), s8[2097152]{0:T(1024)(128)(4,1)S(1)}, s32[]{:S(2)}) async-start(s8[6291456]{0:T(1024)(128)(4,1)} %bitcast.84), calls=%async_computation.2 | async-start | bytes 4194304
  64.8 7.1 %slice-start.1 = ((s8[6291456]{0:T(1024)(128)(4,1)}), s8[4194304]{0:T(1024)(128)(4,1)S(1)}, s32[]{:S(2)}) async-start(s8[6291456]{0:T(1024)(128)(4,1)} %bitcast.84), calls=%async_computation.3 | async-start | bytes 8388608
  68.4 3.5 %copy-start.2 = (bf16[32,128,128]{2,1,0:T(8,128)(2,1)S(1)}, bf16[32,128,128]{2,1,0:T(8,128)(2,1)}, u32[]{:S(2)}) copy-start(bf16[32,128,128]{2,1,0:T(8,128)(2,1)} %gather_fusion.2) | copy-start | bytes 3145732
  73.8 3.9 %slice-start.2 = ((bf16[32,6,128,128]{3,2,1,0:T(8,128)(2,1)}), bf16[32,2,128,128]{3,2,1,0:T(8,128)(2,1)S(1)}, s32[]{:S(2)}) async-start(bf16[32,6,128,128]{3,2,1,0:T(8,128)(2,1)} %param.8), calls=%async_computation.4 | async-start | bytes 4194304 | tf_op jit(solution)/shard_map/slice | solution.py:66
  82.3 3.0 %copy-start.1 = (f32[32,128,128]{1,2,0:T(8,128)S(1)}, f32[32,128,128]{1,2,0:T(8,128)}, u32[]{:S(2)}) copy-start(f32[32,128,128]{1,2,0:T(8,128)} %fusion.4) | copy-start | bytes 6291460
  85.4 4.2 %copy-start.3 = (s32[128,128]{1,0:T(8,128)S(1)}, s32[128,128]{1,0:T(8,128)}, u32[]{:S(2)}) copy-start(s32[128,128]{1,0:T(8,128)} %param.10) | copy-start | bytes 196612
  89.6 72.4 %copy-start.5 = (f32[128]{0:T(128)S(1)}, f32[128]{0:T(128)}, u32[]{:S(2)}) copy-start(f32[128]{0:T(128)} %param.11) | copy-start | bytes 1540
where the time goes:
time: 168 us; the launch traced here: 165 us
  blocking collectives  83.9 us (50%)
  local copies, waits for them, and re-layouts  27.4 us (16%)
  other arithmetic  21.3 us (13%)
  matrix products  20.1 us (12%)
  starting transfers between devices  8.05 us (5%)
  waiting for transfers between devices  3.68 us (2%)
    psum x1, blocking collectives, local(): colmass, boost_mass = lax.psum((mass_part, boost_part), ('rows', 'sub'))  70.3 us
    concatenate x1, other arithmetic, padded(): jnp.concatenate([lax.ppermute(tail, axis, [(i, (i + 1) % count) for i in...  16.4 us
    gather x4, local copies, waits for them, and re-layouts, local(): picked = jnp.take(window, near_index[:, slot_id], axis=0)  14.5 us
    all_to_all x1, blocking collectives, local(): lax.all_to_all(requests, ('rows', 'sub'), split_axis=0, concat_axis=0, ti...  13.6 us
    dot_general x4, matrix products, local(): jnp.einsum('nij,njk->nik', tile_vals[:, slot_id], picked, preferred_eleme...  13.1 us
    dot_general x1, matrix products, local(): jnp.einsum('nij,njk->nik', far_tiles, far_blocks, preferred_element_type=...  4.64 us
    all_to_all x1, starting transfers between devices, local(): lax.all_to_all(found, ('rows', 'sub'), split_axis=0, concat_axis=0, tiled...  4.57 us
    gather x1, local copies, waits for them, and re-layouts, local(): far_blocks = fetched[far_owner, far_slot]  3.88 us
  transfers between devices with their start and end apart: 3, of which 2 were waited for; matrix products, arithmetic and copies ran while one was open for 25% of the time, Pallas kernels for 0%

commit v1 on v0

v1 whole, which is shorter than its diff:
```python
import functools

import jax
import jax.numpy as jnp
from jax import lax
from jax.experimental import pallas as pl
from jax.experimental.pallas import tpu as pltpu
from jax.sharding import PartitionSpec as P

NEAR = 4

eta_step = 2.0
relax_power = 0.5
AXES = ("rows", "sub")


def kernel(
    shards,
    sub,
    far_slots,
    capacity,
    near_ref,
    place_ref,
    asker_ref,
    cpl,
    tiles_hbm,
    req,
    graph,
    cmass,
    out,
    window,
    tiles,
    packed,
    far,
    prod,
    asked,
    asked_s,
    mass_out,
    mass_in,
    new_out,
    new_in,
    graph_t,
    tile_sem,
    asked_sem,
    req_send,
    req_recv,
    near_send,
    near_recv,
    mass_send,
    mass_recv,
    far_send,
    far_recv,
    new_send,
    new_recv,
):
    blocks, size, clusters = cpl.shape
    slots = NEAR + far_slots
    nodes_total = blocks * size * shards
    group = lax.axis_index("groups")
    me = lax.axis_index("rows") * sub + lax.axis_index("sub")

    def where(peer):
        return (group, peer // sub, peer % sub)

    def remote(src, dst, send_sem, recv_sem, peer):
        return pltpu.make_async_remote_copy(
            src_ref=src,
            dst_ref=dst,
            send_sem=send_sem,
            recv_sem=recv_sem,
            device_id=where(peer),
            device_id_type=pl.DeviceIdType.MESH,
        )

    def offset(j):
        return shards // 2 + (1 - 2 * (j % 2)) * ((j + 1) // 2)

    def each_peer(body):
        def step(j, _):
            body((me + offset(j)) % shards)
            return 0

        lax.fori_loop(0, shards - 1, step, 0)

    def each_source(body):
        def step(j, _):
            body((me + shards - offset(j)) % shards)
            return 0

        lax.fori_loop(0, shards - 1, step, 0)

    tile_copy = pltpu.make_async_copy(tiles_hbm, tiles, tile_sem)
    tile_copy.start()

    barrier = pltpu.get_barrier_semaphore()
    each_peer(
        lambda peer: pl.semaphore_signal(
            barrier, inc=1, device_id=where(peer), device_id_type=pl.DeviceIdType.MESH
        )
    )
    asked[me] = req[me]
    pl.semaphore_wait(barrier, shards - 1)

    def req_copy(peer, slot):
        return remote(req.at[peer], asked.at[slot], req_send.at[peer], req_recv.at[slot], peer)

    each_peer(lambda peer: req_copy(peer, me).start())

    below = remote(cpl, window.at[pl.ds(2 * blocks, blocks)], near_send.at[0], near_recv.at[1], me - 1)
    above = remote(cpl, window.at[pl.ds(0, blocks)], near_send.at[1], near_recv.at[0], me + 1)

    @pl.when(me > 0)
    def _():
        below.start()

    @pl.when(me < shards - 1)
    def _():
        above.start()

    def mass_step(b, acc):
        block = cpl[b]
        window[blocks + b] = block
        return acc + jnp.sum(block.astype(jnp.float32).reshape(size // 8, 8, clusters), axis=0)

    acc = lax.fori_loop(0, blocks, mass_step, jnp.zeros((8, clusters), jnp.float32))
    mass_out[...] = jnp.sum(acc, axis=0, keepdims=True)
    mass_in[me] = mass_out[...]

    def mass_copy(peer, slot):
        return remote(mass_out, mass_in.at[slot], mass_send.at[peer], mass_recv.at[slot], peer)

    each_source(lambda peer: req_copy(peer, peer).wait_recv())
    asked_copy = pltpu.make_async_copy(asked, asked_s, asked_sem)
    asked_copy.start()
    asked_copy.wait()

    def far_copy(peer, slot):
        return remote(packed.at[peer], far.at[slot], far_send.at[peer], far_recv.at[slot], peer)

    def pack(peer):
        for s in range(capacity):
            packed[peer, s] = cpl[asked_s[peer, 0, s]]
        far_copy(peer, me).start()

    each_peer(pack)
    for s in range(capacity):
        far[me, s] = cpl[asked_s[me, 0, s]]
    each_peer(lambda peer: mass_copy(peer, me).start())

    graph_f = graph[...].astype(jnp.float32)
    turned = graph_f.T.astype(jnp.bfloat16)
    graph_t[pl.ds(0, clusters)] = turned
    graph_t[pl.ds(clusters, clusters)] = turned
    tile_copy.wait()

    @pl.when(me > 0)
    def _():
        above.wait_recv()

    @pl.when(me < shards - 1)
    def _():
        below.wait_recv()

    def near_step(b, _):
        left = jnp.concatenate([tiles[b * slots + s] for s in range(NEAR)], axis=1)
        right = jnp.concatenate([window[near_ref[b * NEAR + s]] for s in range(NEAR)], axis=0)
        out[b] = jnp.dot(left, right, preferred_element_type=jnp.float32)
        return 0

    lax.fori_loop(0, blocks, near_step, 0)

    def far_products(owner):
        for s in range(capacity):
            prod[owner * capacity + s] = jnp.dot(
                tiles[asker_ref[owner * capacity + s]],
                far[owner, s],
                preferred_element_type=jnp.float32,
            )

    far_products(me)
    each_source(lambda peer: mass_copy(peer, peer).wait_recv())
    colmass = jnp.sum(mass_in[...], axis=0) / nodes_total
    pull = (
        lax.dot_general(
            jnp.broadcast_to(colmass, (8, clusters)),
            graph_f * graph_f,
            (((1,), (1,)), ((), ())),
            precision=lax.Precision.HIGHEST,
            preferred_element_type=jnp.float32,
        )[:1]
        / clusters
    )

    def arrive(owner):
        far_copy(owner, owner).wait_recv()
        far_products(owner)

    each_source(arrive)

    def logit_step(b, acc):
        spread = out[b]
        for f in range(far_slots):
            spread = spread + prod[place_ref[b * far_slots + f]]
        high = spread.astype(jnp.bfloat16)
        low = (spread - high.astype(jnp.float32)).astype(jnp.bfloat16)
        affinity = jnp.dot(
            jnp.concatenate([high, low], axis=1), graph_t[...], preferred_element_type=jnp.float32
        ) / clusters
        logits = jnp.log(cpl[b].astype(jnp.float32)) - eta_step * (pull - 2.0 * affinity)
        out[b] = logits
        return acc + jnp.sum(jnp.exp(logits).reshape(size // 8, 8, clusters), axis=0)

    acc = lax.fori_loop(0, blocks, logit_step, jnp.zeros((8, clusters), jnp.float32))
    new_out[...] = jnp.sum(acc, axis=0, keepdims=True)
    new_in[me] = new_out[...]

    def new_copy(peer, slot):
        return remote(new_out, new_in.at[slot], new_send.at[peer], new_recv.at[slot], peer)

    each_peer(lambda peer: new_copy(peer, me).start())
    each_source(lambda peer: new_copy(peer, peer).wait_recv())
    newmass = jnp.sum(new_in[...], axis=0) / nodes_total
    shift = relax_power * (jnp.log(cmass[...]) - jnp.log(newmass))

    def final_step(b, _):
        shifted = out[b] + shift
        out[b] = shifted - jnp.log(jnp.sum(jnp.exp(shifted), axis=1, keepdims=True))
        return 0

    lax.fori_loop(0, blocks, final_step, 0)

    def drain(peer):
        req_copy(peer, peer).wait_send()
        mass_copy(peer, peer).wait_send()
        far_copy(peer, peer).wait_send()
        new_copy(peer, peer).wait_send()

    each_peer(drain)

    @pl.when(me > 0)
    def _():
        below.wait_send()

    @pl.when(me < shards - 1)
    def _():
        above.wait_send()


def local(coupling, tile_vals, tile_cols, cluster_graph, cluster_mass):
    shards = lax.axis_size(AXES)
    sub = lax.axis_size("sub")
    me = lax.axis_index(AXES)
    blocks, slots = tile_cols.shape
    size = tile_vals.shape[2]
    clusters = coupling.shape[1]
    far_slots = slots - NEAR
    far_count = blocks * far_slots
    capacity = (far_count + shards - 1) // shards
    near_index = (tile_cols[:, :NEAR] - (me * blocks - blocks)).reshape(blocks * NEAR)
    far_cols = tile_cols[:, NEAR:].reshape(far_count)
    owner = far_cols // blocks
    entry = jnp.arange(far_count, dtype=jnp.int32)
    earlier = (owner[:, None] == owner[None, :]) & (entry[:, None] > entry[None, :])
    place = owner * capacity + jnp.sum(earlier.astype(jnp.int32), axis=1)
    held = place[None, :] == jnp.arange(shards * capacity, dtype=jnp.int32)[:, None]
    asker = jnp.sum(
        jnp.where(held, (entry // far_slots * slots + NEAR + entry % far_slots)[None, :], 0), axis=1
    )
    asked = jnp.sum(jnp.where(held, (far_cols % blocks)[None, :], 0), axis=1)
    req = jnp.pad(asked.reshape(shards, 1, capacity), ((0, 0), (0, 0), (0, 128 - capacity)))

    vmem = pl.BlockSpec(memory_space=pltpu.VMEM)
    smem = pl.BlockSpec(memory_space=pltpu.SMEM)
    dma = pltpu.SemaphoreType.DMA
    out = pl.pallas_call(
        functools.partial(kernel, shards, sub, far_slots, capacity),
        out_shape=jax.ShapeDtypeStruct((blocks, size, clusters), jnp.float32),
        in_specs=[smem, smem, smem, vmem, pl.BlockSpec(memory_space=pl.ANY), vmem, vmem, vmem],
        out_specs=vmem,
        scratch_shapes=[
            pltpu.VMEM((3 * blocks, size, clusters), jnp.bfloat16),
            pltpu.VMEM((blocks * slots, size, size), jnp.bfloat16),
            pltpu.VMEM((shards, capacity, size, clusters), jnp.bfloat16),
            pltpu.VMEM((shards, capacity, size, clusters), jnp.bfloat16),
            pltpu.VMEM((shards * capacity, size, clusters), jnp.float32),
            pltpu.VMEM((shards, 1, 128), jnp.int32),
            pltpu.SMEM((shards, 1, 128), jnp.int32),
            pltpu.VMEM((1, clusters), jnp.float32),
            pltpu.VMEM((shards, 1, clusters), jnp.float32),
            pltpu.VMEM((1, clusters), jnp.float32),
            pltpu.VMEM((shards, 1, clusters), jnp.float32),
            pltpu.VMEM((2 * clusters, clusters), jnp.bfloat16),
            dma,
            dma,
            dma((shards,)),
            dma((shards,)),
            dma((2,)),
            dma((2,)),
            dma((shards,)),
            dma((shards,)),
            dma((shards,)),
            dma((shards,)),
            dma((shards,)),
            dma((shards,)),
        ],
        compiler_params=pltpu.CompilerParams(
            collective_id=0, has_side_effects=True, vmem_limit_bytes=48 * 2**20
        ),
        name="partition_step",
    )(
        near_index,
        place,
        asker,
        coupling.reshape(blocks, size, clusters),
        tile_vals.reshape(blocks * slots, size, size),
        req,
        cluster_graph,
        cluster_mass.reshape(1, clusters),
    )
    return out.reshape(blocks * size, clusters)


def solution(mesh):
    return jax.shard_map(
        local,
        mesh=mesh,
        in_specs=(
            P(("groups", "rows", "sub"), None),
            P(("groups", "rows", "sub"), None, None, None),
            P(("groups", "rows", "sub"), None),
            P("groups", None),
            P("groups"),
        ),
        out_specs=P(("groups", "rows", "sub"), None),
        check_vma=False,
    )
```

time: 168 us -> 89.5 us (0.53); the launches traced: 165 us -> 89.3 us
  blocking collectives: 83.9 us -> 0 us
  Pallas kernels: 0 us -> 83 us
  local copies, waits for them, and re-layouts: 27.4 us -> 5.22 us
  other arithmetic: 21.3 us -> 0.99 us
  matrix products: 20.1 us -> 0 us
  starting transfers between devices: 8.05 us -> 0 us
  waiting for transfers between devices: 3.68 us -> 0 us
    pallas_call x0 -> x1, Pallas kernels: none -> 83 us  [local(): pl.pallas_call(functools.partial(kernel, shards, sub, far_slots, capacity...]
    psum x1 -> x0, blocking collectives: 70.3 us -> none  [local(): colmass, boost_mass = lax.psum((mass_part, boost_part), ('rows', 'sub'))]
    dot_general x7 -> x0, matrix products: 20.1 us -> none  [the longest x4 13.1 us: local(): jnp.einsum('nij,njk->nik', tile_vals[:, slot_id], picked, preferred_eleme...]
    gather x6 -> x0, local copies, waits for them, and re-layouts: 19.3 us -> none  [the longest x4 14.5 us: local(): picked = jnp.take(window, near_index[:, slot_id], axis=0)]
    concatenate x3 -> x0, other arithmetic: 16.4 us -> none  [the longest x1 16.4 us: padded(): jnp.concatenate([lax.ppermute(tail, axis, [(i, (i + 1) % count) for i in...]
    all_to_all x1 -> x0, blocking collectives: 13.6 us -> none  [local(): lax.all_to_all(requests, ('rows', 'sub'), split_axis=0, concat_axis=0, ti...]
    all_to_all x1 -> x0, starting transfers between devices: 4.57 us -> none  [local(): lax.all_to_all(found, ('rows', 'sub'), split_axis=0, concat_axis=0, tiled...]
    unnamed x16 -> x7, local copies, waits for them, and re-layouts: 0.03 us -> 4.04 us
  transfers between devices with their start and end apart: 3 -> 0, of which waited for: 2 -> 0; matrix products, arithmetic and copies ran while one was open for 25% -> 0% of each run, Pallas kernels for 0% -> 0%
where the time goes in v1:
time: 89.5 us; the launch traced here: 89.3 us
  Pallas kernels  83 us (93%)
  local copies, waits for them, and re-layouts  5.22 us (6%)
  other arithmetic  0.99 us (1%)
    pallas_call x1, Pallas kernels, local(): pl.pallas_call(functools.partial(kernel, shards, sub, far_slots, capacity...  83 us
    unnamed x7, local copies, waits for them, and re-layouts  4.04 us

profile of v1, /device:TPU:0, one launch (start us, length us, event | category | flops | bytes accessed | tf_op | source)
XLA Modules:
  0.0 89.3 jit_solution(6274207524125794222)
XLA Ops:
  0.0 0.7 slice.7
  0.7 0.7 slice_subtract_fusion
  1.4 0.1 copy.12
  1.5 0.1 reshape.134.near_ref
  1.6 0.1 copy.13
  1.7 0.1 reshape.135
  1.8 0.2 convert_reduce_fusion
  2.0 0.1 select_reduce_fusion
  2.1 0.1 reshape.138
  2.2 0.0 copy-start
  2.2 1.2 %copy-done = bf16[4096,128]{1,0:T(8,128)(2,1)S(1)} copy-done((bf16[4096,128]{1,0:T(8,128)(2,1)S(1)}, bf16[4096,128]{1,0:T(8,128)(2,1)}, u32[]{:S(2)}) %copy-start) | copy-done | bytes 1048600
  3.4 0.0 copy-start.1
  3.4 0.8 copy-done.1
  4.3 0.0 copy-start.2
  4.3 0.7 copy-done.2
  4.9 83.0 %partition_step.1 = f32[32,128,128]{2,1,0:T(8,128)S(1)} custom-call(s32[128]{0:T(128)S(1)} %reshape.134.near_ref, s32[64]{0:T(128)S(1)} %multiply_add_fusion.place_ref, s32[64]{0:T(128)S(1)} %get-tuple-element.6.asker_ref, bf16[32,128,128]{2,1,0:T(8,128)(2,1)S(1)} %bitcast.6, bf16[192,128,128]{2,1,0:T(8,128)(2,1)} %bitcast.8, s32[16,1,128]{2,1,0:T(1,128)S(1)} %pad.4.req, ...), custom_call_target="tpu_custom_call" | custom-call | tf_op jit(solution)/shard_map/partition_step/pallas_call | solution.py:275
  88.0 1.3 %copy.16 = f32[4096,128]{1,0:T(8,128)} copy(f32[4096,128]{1,0:T(8,128)S(1)} %bitcast.5) | data formatting | bytes 4194304
  (3 shorter events, 0.0 us)
Async XLA Ops:
  2.2 1.2 %copy-start = (bf16[4096,128]{1,0:T(8,128)(2,1)S(1)}, bf16[4096,128]{1,0:T(8,128)(2,1)}, u32[]{:S(2)}) copy-start(bf16[4096,128]{1,0:T(8,128)(2,1)} %param.5) | copy-start | bytes 3145732
  3.4 0.8 copy-start.1
  4.3 0.7 copy-start.2

commit v2 on v1

v2 whole, which is shorter than its diff:
```python
import functools

import jax
import jax.numpy as jnp
from jax import lax
from jax.experimental import pallas as pl
from jax.experimental.pallas import tpu as pltpu
from jax.sharding import PartitionSpec as P

NEAR = 4

eta_step = 2.0
relax_power = 0.5
AXES = ("rows", "sub")


def kernel(
    shards,
    sub,
    capacity,
    cpl_hbm,
    tiles_hbm,
    cols_hbm,
    graph_hbm,
    cmass_hbm,
    out_hbm,
    shift_hbm,
    out,
    shift_out,
    own,
    window,
    tiles,
    packed,
    far,
    prod,
    cols,
    cols_s,
    graph,
    cmass,
    table,
    table_s,
    ask_out,
    asked,
    asked_s,
    mass_out,
    mass_in,
    new_out,
    new_in,
    graph_t,
    local_sem,
    ask_sem,
    mass_sem,
    new_sem,
    out_sem,
    near_send,
    near_recv,
    far_send,
    far_recv,
):
    blocks, size, clusters = own.shape
    slots = cols.shape[1]
    far_slots = slots - NEAR
    nodes_total = blocks * size * shards
    group = lax.axis_index("groups")
    me = lax.axis_index("rows") * sub + lax.axis_index("sub")

    def where(peer):
        return (group, peer // sub, peer % sub)

    def remote(src, dst, send_sem, recv_sem, peer):
        return pltpu.make_async_remote_copy(
            src_ref=src,
            dst_ref=dst,
            send_sem=send_sem,
            recv_sem=recv_sem,
            device_id=where(peer),
            device_id_type=pl.DeviceIdType.MESH,
        )

    def offset(j):
        return shards // 2 + (1 - 2 * (j % 2)) * ((j + 1) // 2)

    def each_peer(body):
        def step(j, _):
            body((me + offset(j)) % shards)
            return 0

        lax.fori_loop(0, shards - 1, step, 0)

    def each_source(body):
        def step(j, _):
            body((me + shards - offset(j)) % shards)
            return 0

        lax.fori_loop(0, shards - 1, step, 0)

    other = (me + 1) % shards

    def spread_out(src, dst, sem):
        each_peer(lambda peer: remote(src, dst.at[me], sem.at[0], sem.at[1], peer).start())

    def all_rows(dst, sem):
        rows = dst.at[pl.ds(0, shards - 1)]
        return remote(rows, rows, sem.at[0], sem.at[1], other)

    cols_copy = pltpu.make_async_copy(cols_hbm, cols, local_sem.at[0])
    cols_s_copy = pltpu.make_async_copy(cols_hbm, cols_s, local_sem.at[1])
    own_copy = pltpu.make_async_copy(cpl_hbm, own, local_sem.at[2])
    middle_copy = pltpu.make_async_copy(cpl_hbm, window.at[pl.ds(blocks, blocks)], local_sem.at[3])
    graph_copy = pltpu.make_async_copy(graph_hbm, graph, local_sem.at[4])
    cmass_copy = pltpu.make_async_copy(cmass_hbm, cmass, local_sem.at[5])
    tile_copy = pltpu.make_async_copy(tiles_hbm, tiles, local_sem.at[6])
    for copy in (cols_copy, own_copy, cols_s_copy, graph_copy, cmass_copy, middle_copy, tile_copy):
        copy.start()

    barrier = pltpu.get_barrier_semaphore()
    each_peer(
        lambda peer: pl.semaphore_signal(
            barrier, inc=1, device_id=where(peer), device_id_type=pl.DeviceIdType.MESH
        )
    )

    cols_copy.wait()
    names = cols[...]
    sub_i = lax.broadcasted_iota(jnp.int32, (blocks, blocks), 0)
    lane_i = lax.broadcasted_iota(jnp.int32, (blocks, blocks), 1)
    column = [names[:, NEAR + f : NEAR + f + 1] for f in range(far_slots)]
    row = [
        jnp.sum(jnp.where(sub_i == lane_i, c, 0), axis=0, keepdims=True) for c in column
    ]
    owner_c = [lax.div(c, jnp.int32(blocks)) for c in column]
    owner_r = [lax.div(r, jnp.int32(blocks)) for r in row]
    width = ask_out.shape[1]
    spot = lax.broadcasted_iota(jnp.int32, (blocks, width), 1)
    entry = lax.broadcasted_iota(jnp.int32, (blocks, width), 0)
    asked_row = jnp.zeros((1, width), jnp.int32)
    asker_row = jnp.zeros((1, width), jnp.int32)
    for f in range(far_slots):
        rank_r = jnp.zeros((1, blocks), jnp.int32)
        rank_c = jnp.zeros((blocks, 1), jnp.int32)
        for g in range(far_slots):
            before = sub_i <= lane_i if g < f else sub_i < lane_i
            hit = (owner_c[g] == owner_r[f]) & before
            rank_r = rank_r + jnp.sum(hit.astype(jnp.int32), axis=0, keepdims=True)
            before = lane_i <= sub_i if g < f else lane_i < sub_i
            hit = (owner_c[f] == owner_r[g]) & before
            rank_c = rank_c + jnp.sum(hit.astype(jnp.int32), axis=1, keepdims=True)
        table[pl.ds(1 + f, 1), pl.ds(0, blocks)] = owner_r[f] * capacity + rank_r
        held = (owner_c[f] * capacity + rank_c) == spot
        asked_row = asked_row + jnp.sum(
            jnp.where(held, column[f] - owner_c[f] * blocks, 0), axis=0, keepdims=True
        )
        asker_row = asker_row + jnp.sum(
            jnp.where(held, entry * slots + (NEAR + f), 0), axis=0, keepdims=True
        )
    ask_out[...] = asked_row
    asked[me] = asked_row
    table[pl.ds(0, 1)] = asker_row
    table_copy = pltpu.make_async_copy(table, table_s, local_sem.at[7])
    table_copy.start()

    pl.semaphore_wait(barrier, shards - 1)
    spread_out(ask_out, asked, ask_sem)

    own_copy.wait()
    below = remote(own, window.at[pl.ds(2 * blocks, blocks)], near_send.at[0], near_recv.at[1], me - 1)
    above = remote(own, window.at[pl.ds(0, blocks)], near_send.at[1], near_recv.at[0], me + 1)

    @pl.when(me > 0)
    def _():
        below.start()

    @pl.when(me < shards - 1)
    def _():
        above.start()

    all_rows(asked, ask_sem).wait_recv()
    asked_copy = pltpu.make_async_copy(asked, asked_s, local_sem.at[8])
    asked_copy.start()
    asked_copy.wait()

    def far_copy(peer, slot):
        return remote(packed.at[peer], far.at[slot], far_send.at[peer], far_recv.at[slot], peer)

    def pack(peer):
        for s in range(capacity):
            packed[peer, s] = own[asked_s[peer, 0, me * capacity + s]]
        far_copy(peer, me).start()

    each_peer(pack)
    for s in range(capacity):
        far[me, s] = own[asked_s[me, 0, me * capacity + s]]

    def mass_step(b, acc):
        return acc + jnp.sum(own[b].astype(jnp.float32).reshape(size // 8, 8, clusters), axis=0)

    acc = lax.fori_loop(0, blocks, mass_step, jnp.zeros((8, clusters), jnp.float32))
    mass_out[...] = jnp.sum(acc, axis=0, keepdims=True)
    mass_in[me] = mass_out[...]
    spread_out(mass_out, mass_in, mass_sem)

    graph_copy.wait()
    graph_f = graph[...].astype(jnp.float32)
    turned = graph_f.T.astype(jnp.bfloat16)
    graph_t[pl.ds(0, clusters)] = turned
    graph_t[pl.ds(clusters, clusters)] = turned
    for copy in (tile_copy, cols_s_copy, table_copy, cmass_copy, middle_copy):
        copy.wait()

    def gain(spread):
        high = spread.astype(jnp.bfloat16)
        low = (spread - high.astype(jnp.float32)).astype(jnp.bfloat16)
        return jnp.dot(
            jnp.concatenate([high, low], axis=1), graph_t[...], preferred_element_type=jnp.float32
        ) * (2.0 * eta_step / clusters)

    all_rows(mass_in, mass_sem).wait_recv()
    colmass = jnp.sum(mass_in[...], axis=0) / nodes_total
    pull = (
        lax.dot_general(
            jnp.broadcast_to(colmass, (8, clusters)),
            graph_f * graph_f,
            (((1,), (1,)), ((), ())),
            precision=lax.Precision.HIGHEST,
            preferred_element_type=jnp.float32,
        )[:1]
        / clusters
    )

    @pl.when(me > 0)
    def _():
        above.wait_recv()

    @pl.when(me < shards - 1)
    def _():
        below.wait_recv()

    first = (me - 1) * blocks

    pair = 2 if blocks % 2 == 0 else 1

    def near_step(i, _):
        spread = []
        for u in range(pair):
            b = i * pair + u
            left = jnp.concatenate([tiles[b * slots + s] for s in range(NEAR)], axis=1)
            picked = [jnp.clip(cols_s[b, s] - first, 0, 3 * blocks - 1) for s in range(NEAR)]
            right = jnp.concatenate([window[p] for p in picked], axis=0)
            spread.append(jnp.dot(left, right, preferred_element_type=jnp.float32))
        added = gain(jnp.concatenate(spread, axis=0))
        for u in range(pair):
            b = i * pair + u
            base = jnp.log(own[b].astype(jnp.float32)) - eta_step * pull
            out[b] = base + added[u * size : (u + 1) * size]
        return 0

    lax.fori_loop(0, blocks // pair, near_step, 0)
    all_rows(asked, ask_sem).wait_send()
    all_rows(mass_in, mass_sem).wait_send()

    def far_products(owner):
        for s in range(capacity):
            place = owner * capacity + s
            prod[place] = jnp.dot(
                tiles[table_s[0, place]], far[owner, s], preferred_element_type=jnp.float32
            )

    far_products(me)

    def arrive(owner):
        far_copy(owner, owner).wait_recv()
        far_products(owner)

    each_source(arrive)

    parts = out_sem.shape[0] - 1
    each = blocks // parts
    group_of = next(u for u in (4, 2, 1) if each % u == 0)

    def out_copy(p):
        rows = pl.ds(p * each, each)
        return pltpu.make_async_copy(out.at[rows], out_hbm.at[rows], out_sem.at[p])

    def logit_step(p, i, acc):
        start = p * each + i * group_of
        spread = []
        for u in range(group_of):
            spread.append(prod[table_s[1, start + u]])
            for f in range(1, far_slots):
                spread[u] = spread[u] + prod[table_s[1 + f, start + u]]
        added = gain(jnp.concatenate(spread, axis=0))
        for u in range(group_of):
            logits = out[start + u] + added[u * size : (u + 1) * size]
            out[start + u] = logits
            acc = acc + jnp.sum(jnp.exp(logits).reshape(size // 8, 8, clusters), axis=0)
        return acc

    acc = jnp.zeros((8, clusters), jnp.float32)
    for p in range(parts):
        acc = lax.fori_loop(0, each // group_of, functools.partial(logit_step, p), acc)
        out_copy(p).start()
    new_out[...] = jnp.sum(acc, axis=0, keepdims=True)
    new_in[me] = new_out[...]
    spread_out(new_out, new_in, new_sem)

    each_peer(lambda peer: far_copy(peer, peer).wait_send())

    @pl.when(me > 0)
    def _():
        below.wait_send()

    @pl.when(me < shards - 1)
    def _():
        above.wait_send()

    for p in range(parts):
        out_copy(p).wait()
    all_rows(new_in, new_sem).wait_recv()
    newmass = jnp.sum(new_in[...], axis=0) / nodes_total
    shift_out[...] = relax_power * (jnp.log(cmass[...]) - jnp.log(newmass))
    shift_copy = pltpu.make_async_copy(shift_out, shift_hbm, out_sem.at[parts])
    shift_copy.start()
    shift_copy.wait()
    all_rows(new_in, new_sem).wait_send()


def finish(logits_hbm, shift_hbm, out_hbm, held, shift, in_sem, out_sem):
    blocks = held.shape[0]
    parts = out_sem.shape[0]
    each = blocks // parts
    group_of = next(u for u in (4, 2, 1) if each % u == 0)

    def fetch(p):
        rows = pl.ds(p * each, each)
        return pltpu.make_async_copy(logits_hbm.at[rows], held.at[rows], in_sem.at[p])

    def store(p):
        rows = pl.ds(p * each, each)
        return pltpu.make_async_copy(held.at[rows], out_hbm.at[rows], out_sem.at[p])

    shift_copy = pltpu.make_async_copy(shift_hbm, shift, in_sem.at[parts])
    shift_copy.start()
    for p in range(parts):
        fetch(p).start()
    shift_copy.wait()
    for p in range(parts):
        fetch(p).wait()

        def step(i, _):
            for u in range(group_of):
                b = p * each + i * group_of + u
                shifted = held[b] + shift[...]
                held[b] = shifted - jnp.log(jnp.sum(jnp.exp(shifted), axis=1, keepdims=True))
            return 0

        lax.fori_loop(0, each // group_of, step, 0)
        store(p).start()
    for p in range(parts):
        store(p).wait()


def local(coupling, tile_vals, tile_cols, cluster_graph, cluster_mass):
    shards = lax.axis_size(AXES)
    sub = lax.axis_size("sub")
    blocks, slots = tile_cols.shape
    size = tile_vals.shape[2]
    clusters = coupling.shape[1]
    far_slots = slots - NEAR
    capacity = (blocks * far_slots + shards - 1) // shards
    width = (shards * capacity + 127) // 128 * 128

    parts = next(u for u in (4, 2, 1) if blocks % u == 0)

    hbm = pl.BlockSpec(memory_space=pl.ANY)
    dma = pltpu.SemaphoreType.DMA
    logits, shift = pl.pallas_call(
        functools.partial(kernel, shards, sub, capacity),
        out_shape=(
            jax.ShapeDtypeStruct((blocks, size, clusters), jnp.float32),
            jax.ShapeDtypeStruct((1, clusters), jnp.float32),
        ),
        in_specs=[hbm] * 5,
        out_specs=(hbm, hbm),
        scratch_shapes=[
            pltpu.VMEM((blocks, size, clusters), jnp.float32),
            pltpu.VMEM((1, clusters), jnp.float32),
            pltpu.VMEM((blocks, size, clusters), jnp.bfloat16),
            pltpu.VMEM((3 * blocks, size, clusters), jnp.bfloat16),
            pltpu.VMEM((blocks * slots, size, size), jnp.bfloat16),
            pltpu.VMEM((shards, capacity, size, clusters), jnp.bfloat16),
            pltpu.VMEM((shards, capacity, size, clusters), jnp.bfloat16),
            pltpu.VMEM((shards * capacity, size, clusters), jnp.float32),
            pltpu.VMEM((blocks, slots), jnp.int32),
            pltpu.SMEM((blocks, slots), jnp.int32),
            pltpu.VMEM((clusters, clusters), jnp.int32),
            pltpu.VMEM((1, clusters), jnp.float32),
            pltpu.VMEM((8, width), jnp.int32),
            pltpu.SMEM((8, width), jnp.int32),
            pltpu.VMEM((1, width), jnp.int32),
            pltpu.VMEM((shards, 1, width), jnp.int32),
            pltpu.SMEM((shards, 1, width), jnp.int32),
            pltpu.VMEM((1, clusters), jnp.float32),
            pltpu.VMEM((shards, 1, clusters), jnp.float32),
            pltpu.VMEM((1, clusters), jnp.float32),
            pltpu.VMEM((shards, 1, clusters), jnp.float32),
            pltpu.VMEM((2 * clusters, clusters), jnp.bfloat16),
            dma((9,)),
            dma((2,)),
            dma((2,)),
            dma((2,)),
            dma((parts + 1,)),
            dma((2,)),
            dma((2,)),
            dma((shards,)),
            dma((shards,)),
        ],
        compiler_params=pltpu.CompilerParams(
            collective_id=0, has_side_effects=True, vmem_limit_bytes=56 * 2**20
        ),
        name="partition_step",
    )(
        coupling.reshape(blocks, size, clusters),
        tile_vals.reshape(blocks * slots, size, size),
        tile_cols,
        cluster_graph,
        cluster_mass.reshape(1, clusters),
    )
    out = pl.pallas_call(
        finish,
        out_shape=jax.ShapeDtypeStruct((blocks, size, clusters), jnp.float32),
        in_specs=[hbm, hbm],
        out_specs=hbm,
        scratch_shapes=[
            pltpu.VMEM((blocks, size, clusters), jnp.float32),
            pltpu.VMEM((1, clusters), jnp.float32),
            dma((parts + 1,)),
            dma((parts,)),
        ],
        compiler_params=pltpu.CompilerParams(vmem_limit_bytes=56 * 2**20),
        name="normalise",
    )(logits, shift)
    return out.reshape(blocks * size, clusters)


def solution(mesh):
    return jax.shard_map(
        local,
        mesh=mesh,
        in_specs=(
            P(("groups", "rows", "sub"), None),
            P(("groups", "rows", "sub"), None, None, None),
            P(("groups", "rows", "sub"), None),
            P("groups", None),
            P("groups"),
        ),
        out_specs=P(("groups", "rows", "sub"), None),
        check_vma=False,
    )
```

time: 89.5 us -> 85.3 us (0.953)
  local copies, waits for them, and re-layouts: 5.22 us -> 1.37 us
  other arithmetic: 0.99 us -> 0 us
    unnamed x7 -> x1, local copies, waits for them, and re-layouts: 4.04 us -> 1.37 us
    pallas_call x1 -> x2, Pallas kernels: 83 us -> 83.6 us  [the longest x1 80.4 us: local(): pl.pallas_call(functools.partial(kernel, shards, sub, capacity), out_shap...]
where the time goes in v2:
time: 85.3 us; the launch traced here: 85 us
  Pallas kernels  83.6 us (98%)
  local copies, waits for them, and re-layouts  1.37 us (2%)
    pallas_call x1, Pallas kernels, local(): pl.pallas_call(functools.partial(kernel, shards, sub, capacity), out_shap...  80.4 us
    pallas_call x1, Pallas kernels, local(): pl.pallas_call(finish, out_shape=jax.ShapeDtypeStruct((blocks, size, clus...  3.19 us

profile of v2, /device:TPU:0, one launch (start us, length us, event | category | flops | bytes accessed | tf_op | source)
XLA Modules:
  0.0 85.0 jit_solution(9306353380915777269)
XLA Ops:
  0.0 1.4 %copy.6.cols_hbm = s32[32,6]{1,0:T(8,128)} copy(s32[32,6]{0,1:T(8,128)} %param.7) | data formatting | bytes 1536 | tf_op args[2]
  1.4 80.4 %partition_step.1 = (f32[32,128,128]{2,1,0:T(8,128)}, f32[1,128]{1,0:T(1,128)}) custom-call(bf16[32,128,128]{2,1,0:T(8,128)(2,1)} %bitcast.5, bf16[192,128,128]{2,1,0:T(8,128)(2,1)} %bitcast.4, s32[32,6]{1,0:T(8,128)} %copy.6.cols_hbm, s32[128,128]{1,0:T(8,128)} %graph_hbm.1, f32[1,128]{1,0:T(1,128)} %bitcast.6), custom_call_target="tpu_custom_call" | custom-call | tf_op jit(solution)/shard_map/partition_step/pallas_call | solution.py:376
  81.8 3.2 %normalise.1 = f32[32,128,128]{2,1,0:T(8,128)} custom-call(f32[32,128,128]{2,1,0:T(8,128)} %get-tuple-element.7.logits_hbm, f32[1,128]{1,0:T(1,128)} %get-tuple-element.8.shift_hbm), custom_call_target="tpu_custom_call" | custom-call | tf_op jit(solution)/shard_map/normalise/pallas_call | solution.py:428

commit v3 on v2

--- a/solution.py
+++ b/solution.py
@@ -58,7 +58,7 @@
     far_recv,
 ):
     blocks, size, clusters = own.shape
-    slots = cols.shape[1]
+    slots = cols.shape[0]
     far_slots = slots - NEAR
     nodes_total = blocks * size * shards
     group = lax.axis_index("groups")
@@ -77,19 +77,22 @@
             device_id_type=pl.DeviceIdType.MESH,
         )
 
-    def offset(j):
-        return shards // 2 + (1 - 2 * (j % 2)) * ((j + 1) // 2)
+    half = shards // 2
+    mine = me // half * half
+    theirs = half - mine
 
     def each_peer(body):
         def step(j, _):
-            body((me + offset(j)) % shards)
+            other_half = 1 - j % 2
+            body(mine + other_half * (theirs - mine) + (me + (j + 1) // 2) % half)
             return 0
 
         lax.fori_loop(0, shards - 1, step, 0)
 
     def each_source(body):
         def step(j, _):
-            body((me + shards - offset(j)) % shards)
+            other_half = 1 - j % 2
+            body(mine + other_half * (theirs - mine) + (me + half - (j + 1) // 2) % half)
             return 0
 
         lax.fori_loop(0, shards - 1, step, 0)
@@ -124,9 +127,9 @@
     names = cols[...]
     sub_i = lax.broadcasted_iota(jnp.int32, (blocks, blocks), 0)
     lane_i = lax.broadcasted_iota(jnp.int32, (blocks, blocks), 1)
-    column = [names[:, NEAR + f : NEAR + f + 1] for f in range(far_slots)]
-    row = [
-        jnp.sum(jnp.where(sub_i == lane_i, c, 0), axis=0, keepdims=True) for c in column
+    row = [names[NEAR + f : NEAR + f + 1] for f in range(far_slots)]
+    column = [
+        jnp.sum(jnp.where(sub_i == lane_i, r, 0), axis=1, keepdims=True) for r in row
     ]
     owner_c = [lax.div(c, jnp.int32(blocks)) for c in column]
     owner_r = [lax.div(r, jnp.int32(blocks)) for r in row]
@@ -159,10 +162,18 @@
     table_copy = pltpu.make_async_copy(table, table_s, local_sem.at[7])
     table_copy.start()
 
+    own_copy.wait()
+
+    def mass_step(b, acc):
+        return acc + jnp.sum(own[b].astype(jnp.float32).reshape(size // 8, 8, clusters), axis=0)
+
+    acc = lax.fori_loop(0, blocks, mass_step, jnp.zeros((8, clusters), jnp.float32))
+    mass_out[...] = jnp.sum(acc, axis=0, keepdims=True)
+    mass_in[me] = mass_out[...]
+
     pl.semaphore_wait(barrier, shards - 1)
     spread_out(ask_out, asked, ask_sem)
-
-    own_copy.wait()
+    spread_out(mass_out, mass_in, mass_sem)
     below = remote(own, window.at[pl.ds(2 * blocks, blocks)], near_send.at[0], near_recv.at[1], me - 1)
     above = remote(own, window.at[pl.ds(0, blocks)], near_send.at[1], near_recv.at[0], me + 1)
 
@@ -190,14 +201,6 @@
     each_peer(pack)
     for s in range(capacity):
         far[me, s] = own[asked_s[me, 0, me * capacity + s]]
-
-    def mass_step(b, acc):
-        return acc + jnp.sum(own[b].astype(jnp.float32).reshape(size // 8, 8, clusters), axis=0)
-
-    acc = lax.fori_loop(0, blocks, mass_step, jnp.zeros((8, clusters), jnp.float32))
-    mass_out[...] = jnp.sum(acc, axis=0, keepdims=True)
-    mass_in[me] = mass_out[...]
-    spread_out(mass_out, mass_in, mass_sem)
 
     graph_copy.wait()
     graph_f = graph[...].astype(jnp.float32)
@@ -244,7 +247,7 @@
         for u in range(pair):
             b = i * pair + u
             left = jnp.concatenate([tiles[b * slots + s] for s in range(NEAR)], axis=1)
-            picked = [jnp.clip(cols_s[b, s] - first, 0, 3 * blocks - 1) for s in range(NEAR)]
+            picked = [jnp.clip(cols_s[s, b] - first, 0, 3 * blocks - 1) for s in range(NEAR)]
             right = jnp.concatenate([window[p] for p in picked], axis=0)
             spread.append(jnp.dot(left, right, preferred_element_type=jnp.float32))
         added = gain(jnp.concatenate(spread, axis=0))
@@ -390,8 +393,8 @@
             pltpu.VMEM((shards, capacity, size, clusters), jnp.bfloat16),
             pltpu.VMEM((shards, capacity, size, clusters), jnp.bfloat16),
             pltpu.VMEM((shards * capacity, size, clusters), jnp.float32),
-            pltpu.VMEM((blocks, slots), jnp.int32),
-            pltpu.SMEM((blocks, slots), jnp.int32),
+            pltpu.VMEM((slots, blocks), jnp.int32),
+            pltpu.SMEM((slots, blocks), jnp.int32),
             pltpu.VMEM((clusters, clusters), jnp.int32),
             pltpu.VMEM((1, clusters), jnp.float32),
             pltpu.VMEM((8, width), jnp.int32),
@@ -421,7 +424,7 @@
     )(
         coupling.reshape(blocks, size, clusters),
         tile_vals.reshape(blocks * slots, size, size),
-        tile_cols,
+        tile_cols.T,
         cluster_graph,
         cluster_mass.reshape(1, clusters),
     )

time: 85.3 us -> 75.9 us (0.89)
  Pallas kernels: 83.6 us -> 75.7 us
  local copies, waits for them, and re-layouts: 1.37 us -> 0 us
    pallas_call x1, Pallas kernels: 80.4 us -> 72.5 us  [local(): pl.pallas_call(functools.partial(kernel, shards, sub, capacity), out_shap...]
    unnamed x1 -> x0, local copies, waits for them, and re-layouts: 1.37 us -> none
where the time goes in v3:
time: 75.9 us; the launch traced here: 75.7 us
  Pallas kernels  75.7 us (100%)
    pallas_call x1, Pallas kernels, local(): pl.pallas_call(functools.partial(kernel, shards, sub, capacity), out_shap...  72.5 us
    pallas_call x1, Pallas kernels, local(): pl.pallas_call(finish, out_shape=jax.ShapeDtypeStruct((blocks, size, clus...  3.19 us

profile of v3, /device:TPU:0, one launch (start us, length us, event | category | flops | bytes accessed | tf_op | source)
XLA Modules:
  0.0 75.7 jit_solution(5216532528261314241)
XLA Ops:
  0.0 72.5 %partition_step.1 = (f32[32,128,128]{2,1,0:T(8,128)}, f32[1,128]{1,0:T(1,128)}) custom-call(bf16[32,128,128]{2,1,0:T(8,128)(2,1)} %bitcast.6, bf16[192,128,128]{2,1,0:T(8,128)(2,1)} %bitcast.5, s32[6,32]{1,0:T(8,128)} %bitcast.7, s32[128,128]{1,0:T(8,128)} %graph_hbm.1, f32[1,128]{1,0:T(1,128)} %bitcast.8), custom_call_target="tpu_custom_call" | custom-call | tf_op jit(solution)/shard_map/partition_step/pallas_call | solution.py:379
  72.5 3.2 %normalise.1 = f32[32,128,128]{2,1,0:T(8,128)} custom-call(f32[32,128,128]{2,1,0:T(8,128)} %get-tuple-element.7.logits_hbm, f32[1,128]{1,0:T(1,128)} %get-tuple-element.8.shift_hbm), custom_call_target="tpu_custom_call" | custom-call | tf_op jit(solution)/shard_map/normalise/pallas_call | solution.py:431
